TPU v7x, 32 devices: a whole 2x2x4 slice. The times are simulated.
32 devices in a mesh: dp: 4 (over y, x), tm: 8 (over z, core).
Axes of the slice: x: 2, y: 2, z: 4, core: 2. Of those that a mesh axis runs over, the one named last changes fastest.
Arguments:
- records: bfloat16 [4, 1024, 1024], P('dp', 'tm'), may hold values from -6 to 6
- x_weight: bfloat16 [1024, 512], replicated, may hold values from -0.1875 to 0.1875
- bc_weight: bfloat16 [1024, 256], replicated, may hold values from -0.1875 to 0.1875
- decay_codes: int32 [4, 1024, 8], P('dp', 'tm'), may hold values from 0 to 524
- out_grad: bfloat16 [4, 1024, 512], P('dp', 'tm'), may hold values from -6 to 6
Outputs:
- y_out: bfloat16 [4, 1024, 512], P('dp', 'tm')
- x_grad: float32 [1024, 512], P('tm')
- bc_grad: float32 [1024, 256], P('tm')
All inputs are finite; a program needn't handle non-finite values.
Results may differ from a plain program's by a relative error of at most 0.0085.
Values sent between devices are 32-bit elements; how exact they have to be, the bound alone decides.
A program may use at most 64 MiB of HBM per device.

v0:
```python
import jax
import jax.numpy as jnp
from jax import lax
from jax.sharding import PartitionSpec as P

SPAN = 128


highest = lax.Precision.HIGHEST


def entering(part, axis, combine, identity, reverse):
    count = lax.axis_size(axis)
    place = lax.axis_index(axis)
    ahead = count - 1 - place if reverse else place
    gathered = jax.tree.map(lambda a: lax.all_gather(a, axis), part)
    state = jax.tree.map(lambda a, e: jnp.zeros_like(a) + jnp.asarray(e, a.dtype), part, identity)

    def one(turn, state):
        source = count - 1 - turn if reverse else turn
        return combine(
            state, jax.tree.map(lambda a: lax.dynamic_index_in_dim(a, source, 0, False), gathered)
        )

    return lax.fori_loop(0, ahead, one, state)


def span_kernel(log_decay):
    running = jnp.cumsum(log_decay, axis=1)
    length = log_decay.shape[1]
    causal = lax.broadcasted_iota(jnp.int32, (length, length), 0) >= lax.broadcasted_iota(
        jnp.int32, (length, length), 1
    )
    causal = causal[None, None, :, :]
    heads_first = jnp.transpose(running, (0, 2, 1))
    gaps = heads_first[:, :, :, None] - heads_first[:, :, None, :]
    kernel = jnp.where(causal, jnp.exp(jnp.where(causal, gaps, 0.0)), 0.0)
    return (running, kernel)


def block_scores(readout, inject):
    return jnp.einsum(
        "rtn,rsn->rts",
        readout.astype(jnp.bfloat16),
        inject.astype(jnp.bfloat16),
        preferred_element_type=jnp.float32,
    )


def forward_span(carry_state, pieces):
    mixer_f, inject, readout, cot_heads, log_decay = pieces
    running, kernel = span_kernel(log_decay)
    scores = block_scores(readout, inject)
    mixing = kernel * scores[:, None, :, :]
    decayed = jnp.exp(running)
    within = jnp.einsum("rhts,rshp->rthp", mixing, mixer_f, precision=highest)
    carried = decayed[..., None] * jnp.einsum(
        "rhpn,rtn->rthp", carry_state, readout, precision=highest
    )
    pair_dots = jnp.einsum("rthp,rshp->rhts", cot_heads, mixer_f, precision=highest)
    grad_read = jnp.einsum("rhts,rsn->rtn", kernel * pair_dots, inject, precision=highest)
    grad_read = grad_read + jnp.einsum(
        "rthp,rhpn->rtn", decayed[..., None] * cot_heads, carry_state, precision=highest
    )
    to_end = jnp.exp(running[:, -1:, :] - running)
    new_state = jnp.exp(running[:, -1, :])[:, :, None, None] * carry_state
    new_state = new_state + jnp.einsum(
        "rshp,rsn->rhpn", to_end[..., None] * mixer_f, inject, precision=highest
    )
    return (new_state, (within + carried, grad_read))


def reverse_span(adjoint, pieces):
    mixer_f, inject, readout, cot_heads, log_decay = pieces
    running, kernel = span_kernel(log_decay)
    scores = block_scores(readout, inject)
    mixing = kernel * scores[:, None, :, :]
    pair_dots = jnp.einsum("rthp,rshp->rhts", cot_heads, mixer_f, precision=highest)
    to_end = jnp.exp(running[:, -1:, :] - running)
    grad_mixer = jnp.einsum("rhts,rthp->rshp", mixing, cot_heads, precision=highest)
    grad_mixer = grad_mixer + to_end[..., None] * jnp.einsum(
        "rhpn,rsn->rshp", adjoint, inject, precision=highest
    )
    grad_inject = jnp.einsum("rhts,rtn->rsn", kernel * pair_dots, readout, precision=highest)
    grad_inject = grad_inject + jnp.einsum(
        "rshp,rhpn->rsn", to_end[..., None] * mixer_f, adjoint, precision=highest
    )
    new_adjoint = jnp.exp(running[:, -1, :])[:, :, None, None] * adjoint
    new_adjoint = new_adjoint + jnp.einsum(
        "rthp,rtn->rhpn", jnp.exp(running)[..., None] * cot_heads, readout, precision=highest
    )
    return (new_adjoint, (grad_mixer, grad_inject))


def to_blocks(array, frames):
    return array.reshape((frames // SPAN, 1, SPAN) + array.shape[1:])


def combine_pair(earlier, later_one):
    return (earlier[0] * later_one[0], later_one[0][:, :, None, None] * earlier[1] + later_one[1])


def body(records, x_weight, bc_weight, decay_codes, out_grad):
    signal = records[0]
    codes = decay_codes[0]
    frames_dev, model_dim = signal.shape
    head_count = codes.shape[1]
    mixer_dim = x_weight.shape[1]
    head_size = mixer_dim // head_count
    state_size = bc_weight.shape[1] // 2
    tm_count = lax.axis_size("tm")
    groups = lax.axis_size("dp")
    out_scale = (state_size * frames_dev * tm_count) ** (-0.5)
    grad_scale = (groups * frames_dev * tm_count) ** (-0.5)
    decay_unit = 1.0 / (32.0 * frames_dev * tm_count)
    mixer_in = jnp.dot(signal, x_weight, preferred_element_type=jnp.float32).astype(jnp.bfloat16)
    state_proj = jnp.dot(signal, bc_weight, preferred_element_type=jnp.float32).astype(jnp.bfloat16)
    log_decay = -decay_unit * codes.astype(jnp.float32)
    cotangent = out_grad[0].astype(jnp.float32) * out_scale
    mixer_f = mixer_in.astype(jnp.float32).reshape(frames_dev, head_count, head_size)
    inject = state_proj[:, :state_size].astype(jnp.float32)
    readout = state_proj[:, state_size:].astype(jnp.float32)
    cot_heads = cotangent.reshape(frames_dev, head_count, head_size)
    blocks = (
        to_blocks(mixer_f, frames_dev),
        to_blocks(inject, frames_dev),
        to_blocks(readout, frames_dev),
        to_blocks(cot_heads, frames_dev),
        to_blocks(log_decay, frames_dev),
    )
    zero_state = jnp.zeros((1, head_count, head_size, state_size), jnp.float32)
    end_state, (local_out, local_read) = lax.scan(forward_span, zero_state, blocks)
    start_adjoint, (local_grad, local_inject) = lax.scan(
        reverse_span, zero_state, blocks, reverse=True
    )
    running = jnp.cumsum(log_decay, axis=0)
    device_log = running[-1]
    identity = (jnp.ones((1, head_count), jnp.float32), zero_state)
    carry_in = entering(
        (jnp.exp(device_log)[None], end_state), "tm", combine_pair, identity, False
    )[1][0]
    adjoint_in = entering(
        (jnp.exp(device_log)[None], start_adjoint), "tm", combine_pair, identity, True
    )[1][0]
    decayed = jnp.exp(running)
    to_end = jnp.exp(device_log[None] - running)
    output = local_out.reshape(frames_dev, head_count, head_size)
    output = output + decayed[..., None] * jnp.einsum(
        "hpn,tn->thp", carry_in, readout, precision=highest
    )
    grad_read = local_read.reshape(frames_dev, state_size)
    grad_read = grad_read + jnp.einsum(
        "thp,hpn->tn", decayed[..., None] * cot_heads, carry_in, precision=highest
    )
    grad_mixer = local_grad.reshape(frames_dev, head_count, head_size)
    grad_mixer = grad_mixer + to_end[..., None] * jnp.einsum(
        "hpn,tn->thp", adjoint_in, inject, precision=highest
    )
    grad_inject = local_inject.reshape(frames_dev, state_size)
    grad_inject = grad_inject + jnp.einsum(
        "thp,hpn->tn", to_end[..., None] * mixer_f, adjoint_in, precision=highest
    )
    grad_mix = grad_mixer.reshape(frames_dev, mixer_dim).astype(jnp.bfloat16)
    grad_proj = jnp.concatenate([grad_inject, grad_read], axis=1).astype(jnp.bfloat16)
    grad_cat = jnp.concatenate([grad_mix, grad_proj], axis=1)
    grad_share = lax.psum_scatter(
        lax.dot_general(
            signal, grad_cat, (((0,), (0,)), ((), ())), preferred_element_type=jnp.float32
        ),
        "tm",
        scatter_dimension=0,
        tiled=True,
    )
    grad_share = lax.psum(grad_share, "dp")
    grad_share = grad_share * grad_scale
    y_out = output.reshape(frames_dev, mixer_dim).astype(jnp.bfloat16)[None]
    return (y_out, grad_share[:, :mixer_dim], grad_share[:, mixer_dim:])


def solution(mesh):
    return jax.shard_map(
        body,
        mesh=mesh,
        in_specs=(P("dp", "tm", None), P(), P(), P("dp", "tm", None), P("dp", "tm", None)),
        out_specs=(P("dp", "tm", None), P("tm", None), P("tm", None)),
        check_vma=False,
    )
```

profile of v0, /device:TPU:0, one launch (start us, length us, event | category | flops | bytes accessed | tf_op | source)
XLA Modules:
  0.0 178.9 jit_solution(16157964880768725802)
XLA Ops:
  7.2 0.0 copy-start
  7.2 0.0 copy-start.2
  7.2 0.0 copy-start.1
  7.2 0.0 all-gather.7.cloned.1.call-start
  7.2 0.8 fusion.69
  8.1 0.1 copy.70
  8.2 0.2 reduce_window_sum.27
  8.4 0.1 copy.74
  8.5 0.2 reduce_window_sum.29
  8.8 0.1 copy.82
  9.0 0.1 fusion.61
  9.1 0.1 copy.76
  9.2 0.0 copy-done.2
  9.2 0.0 copy-done.1
  9.2 0.2 convolution_convert_fusion.1
  9.5 0.0 copy-done
  9.5 0.0 copy-start.3
  9.5 0.3 convert_multiply_fusion
  9.8 0.1 copy.77
  10.0 1.0 convolution_add_fusion.1
  10.9 0.0 all-gather.7.cloned.1.call-update
  10.9 0.0 all-gather.9.cloned.1.call-start
  11.0 0.1 copy.79
  11.2 0.1 convert_multiply_fusion.2
  11.3 1.0 convolution_add_fusion
  12.2 0.0 all-gather.9.cloned.1.call-update
  12.2 0.0 reduce-scatter.2.cloned.1.call-start
  12.3 0.1 copy.69
  12.5 0.1 copy.83
  12.6 13.5 %all-gather.3 = f32[8,1,8]{2,1,0:T(1,128)S(1)} all-gather(f32[1,1,8]{2,1,0:T(1,128)S(1)} %get-tuple-element.267), channel_id=2, replica_groups=mesh['dp'=4,'tm'=8] {'tm'}, dimensions={0}, use_global_device_ids=true | all-gather | bytes 288 | tf_op jit(solution)/shard_map/all_gather | solution.py:16
  26.1 0.3 fusion.2
  26.4 0.4 convolution_bitcast_fusion.4
  26.8 0.4 convolution_bitcast_fusion.6
  27.2 0.7 fusion
  27.9 0.1 fusion.54
  28.0 0.8 fusion.4
  28.8 14.1 %all-gather.7.cloned.1.call-done = f32[64,64,128]{2,1,0:T(8,128)} async-done(((f32[8,64,128]{2,1,0:T(8,128)}), f32[64,64,128]{2,1,0:T(8,128)}) %all-gather.7.cloned.1.call-update) | async-done | bytes 2097168 | tf_op jit(solution)/shard_map/all_gather | solution.py:16
  42.9 30.2 %all-gather.9.cloned.1.call-done = f32[64,64,128]{2,1,0:T(8,128)} async-done(((f32[8,64,128]{2,1,0:T(8,128)}), f32[64,64,128]{2,1,0:T(8,128)}) %all-gather.9.cloned.1.call-update) | async-done | bytes 2097168 | tf_op jit(solution)/shard_map/all_gather | solution.py:16
  73.1 7.7 %while.17 = (s32[]{:T(128)}, f32[1,8,64,128]{3,2,1,0:T(8,128)S(1)}, s32[]{:T(128)}, f32[8,1,8]{2,1,0:T(1,128)S(1)}, f32[8,1,8,64,128]{4,3,2,1,0:T(8,128)}, /*index=5*/s32[]{:T(128)}, s32[]{:T(128)}, s32[]{:T(128)}, s32[]{:T(128)}) while((s32[]{:T(128)}, f32[1,8,64,128]{3,2,1,0:T(8,128)S(1)}, s32[]{:T(128)}, f32[8,1,8]{2,1,0:T(1,128)S(1)}, ...), condition=%wide.region_5.6_spmd, body=%wide.region_4.5_spmd.sunk | while | flops 131078 | bytes 786683 | solution.py:25
  73.2 1.1 bitcast_add_fusion.5
  74.3 1.1 bitcast_add_fusion.5
  75.4 1.1 bitcast_add_fusion.5
  76.5 1.1 bitcast_add_fusion.5
  77.6 1.1 bitcast_add_fusion.5
  78.7 1.1 bitcast_add_fusion.5
  79.8 1.1 bitcast_add_fusion.5
  80.9 0.6 convolution_bitcast_fusion.5
  81.5 0.3 fusion.10
  81.8 0.6 convolution_bitcast_fusion.3
  82.3 0.2 fusion.14
  82.6 0.2 fusion.13
  82.8 2.2 %convolution_bitcast_fusion = f32[1024,768]{0,1:T(8,128)} fusion(bf16[1,128,1024]{2,1,0:T(8,128)(2,1)S(1)} %copy-done.1, bf16[128,128]{0,1:T(8,128)(2,1)S(1)} %fusion.14, bf16[128,128]{0,1:T(8,128)(2,1)S(1)} %fusion.13, bf16[128,512]{0,1:T(8,128)(2,1)S(1)} %bitcast.146), kind=kOutput, calls=%fused_computation.4 | convolution fusion | flops 201916416 | bytes 3604480 | tf_op jit(solution)/shard_map/dot_general | solution.py:167
  85.0 0.0 reduce-scatter.2.cloned.1.call-update
  85.1 0.0 all-reduce.2.cloned.1.call-start
  85.1 0.3 fusion.6
  85.4 38.3 %reduce-scatter.2.cloned.1.call-done = f32[128,768]{0,1:T(8,128)} async-done(((f32[1024,768]{0,1:T(8,128)}), f32[128,768]{0,1:T(8,128)}) %reduce-scatter.2.cloned.1.call-update) | async-done | bytes 393232 | tf_op jit(solution)/shard_map/reduce_scatter | solution.py:166
  123.7 0.0 all-reduce.2.cloned.1.call-update
  123.7 0.7 fusion.8
  124.5 0.3 fusion.9
  124.8 0.8 copy.84
  125.5 44.2 %all-reduce.2.cloned.1.call-done = f32[128,768]{0,1:T(8,128)} async-done(((f32[128,768]{0,1:T(8,128)}), f32[128,768]{0,1:T(8,128)}) %all-reduce.2.cloned.1.call-update) | async-done | bytes 393232 | tf_op jit(solution)/shard_map/psum | solution.py:174
  169.7 1.0 broadcast_multiply_fusion
  170.8 0.8 copy.85
  171.6 0.8 copy.86
  (24 shorter events, 0.5 us)
Async XLA Ops:
  7.2 2.3 %copy-start = (bf16[1024,512]{1,0:T(8,128)(2,1)S(1)}, bf16[1024,512]{1,0:T(8,128)(2,1)}, u32[]{:S(2)}) copy-start(bf16[1024,512]{1,0:T(8,128)(2,1)} %param.10) | copy-start | bytes 3145732
  7.2 2.0 %copy-start.2 = (bf16[1024,256]{1,0:T(8,128)(2,1)S(1)}, bf16[1024,256]{1,0:T(8,128)(2,1)}, u32[]{:S(2)}) copy-start(bf16[1024,256]{1,0:T(8,128)(2,1)} %param.11) | copy-start | bytes 1572868
  7.2 2.0 %copy-start.1 = (bf16[1,128,1024]{2,1,0:T(8,128)(2,1)S(1)}, bf16[1,128,1024]{2,1,0:T(8,128)(2,1)}, u32[]{:S(2)}) copy-start(bf16[1,128,1024]{2,1,0:T(8,128)(2,1)} %param.9) | copy-start | bytes 786436
  7.2 35.7 %all-gather.7.cloned.1.call-start = ((), (), s32[]{:S(2)}) async-start(), calls=%async_computation.3 | async-start | bytes 2359296 | tf_op jit(solution)/shard_map/all_gather | solution.py:16
  9.5 1.6 copy-start.3
  10.9 62.2 %all-gather.9.cloned.1.call-start = ((), (), s32[]{:S(2)}) async-start(), calls=%async_computation.4 | async-start | bytes 2359296 | tf_op jit(solution)/shard_map/all_gather | solution.py:16
  12.2 111.5 %reduce-scatter.2.cloned.1.call-start = ((), (), s32[]{:S(2)}) async-start(), calls=%async_computation.1 | async-start | bytes 3538944 | tf_op jit(solution)/shard_map/reduce_scatter | solution.py:166
  85.1 84.7 %all-reduce.2.cloned.1.call-start = ((), (), s32[]{:S(2)}) async-start(), calls=%async_computation.2 | async-start | bytes 786432 | tf_op jit(solution)/shard_map/psum | solution.py:174
Sparse Core Ops, SparseCore 0:
  11.1 31.7 all-gather.6
  44.5 28.5 all-gather.8
  85.2 38.4 reduce-scatter.1
  126.5 43.1 all-reduce.1
where the time goes:
time: 179 us
  waiting for transfers between devices  127 us (71%)
  between operations  14.1 us (8%)
  blocking collectives  13.5 us (8%)
  matrix products  10.5 us (6%)
  other arithmetic  9.79 us (5%)
  local copies, waits for them, and re-layouts  3.76 us (2%)
    all_gather x2, waiting for transfers between devices, entering(): gathered = jax.tree.map(lambda a: lax.all_gather(a, axis), part)  44.3 us
    psum x1, waiting for transfers between devices, body(): grad_share = lax.psum(grad_share, 'dp')  44.2 us
    reduce_scatter x1, waiting for transfers between devices, body(): lax.psum_scatter(lax.dot_general(signal, grad_cat, (((0,), (0,)), ((), ()...  38.3 us
    all_gather x1, blocking collectives, entering(): gathered = jax.tree.map(lambda a: lax.all_gather(a, axis), part)  13.5 us
    add x7, other arithmetic, combine_pair(): later_one[0][:, :, None, None] * earlier[1] + later_one[1]  7.43 us
  transfers between devices with their start and end apart: 4, of which 4 were waited for; matrix products, arithmetic and copies ran while one was open for 3% of the time, Pallas kernels for 0%

commit v1 on v0

v1 whole, which is shorter than its diff:
```python
import functools

import jax
import jax.numpy as jnp
from jax import lax
from jax.experimental import pallas as pl
from jax.experimental.pallas import tpu as pltpu
from jax.sharding import PartitionSpec as P

MESH = pl.DeviceIdType.MESH
CHUNKS = 4
f32 = jnp.float32
bf16 = jnp.bfloat16


def dot(a, b, left=1, right=0):
    return lax.dot_general(
        a, b, (((left,), (right,)), ((), ())), preferred_element_type=f32
    )


def kernel(
    groups, tm, rec_ref, xw_ref, bw_ref, code_ref, og_ref, y_ref, out_ref,
    rec_all, carry, adj, ends, starts, sent_f, sent_b, keep,
    gt, gall, pt, pbuf, qs, rbuf, fin, ylocal, glocal,
    rec_s, rec_r, f_s, f_r, b_s, b_r, g_s, g_r, c_s, c_r, z_s, z_r, o_s, o_r,
):
    frames, heads = code_ref.shape
    width = xw_ref.shape[1]
    head = width // heads
    state = bw_ref.shape[1] // 2
    rows = out_ref.shape[2]
    block = out_ref.shape[1]
    chips = tm // 2
    unit = 1.0 / (32.0 * frames * tm)
    scale = (state * frames * tm) ** (-0.5)

    d = lax.axis_index("dp")
    i = lax.axis_index("tm")
    z = i // 2
    core = i % 2
    partner = i + 1 - 2 * core
    other = i - 1 + 2 * core
    has_other = jnp.logical_and(other >= 0, other < tm)

    barrier = pltpu.get_barrier_semaphore()

    def greet(dp_to, tm_to):
        pl.semaphore_signal(barrier, inc=1, device_id=(dp_to, tm_to), device_id_type=MESH)

    for k in range(1, groups):
        greet(lax.rem(d + k, groups), i)
    for k in range(1, chips):
        greet(d, lax.rem(z + k, chips) * 2 + core)
    greet(d, partner)

    @pl.when(has_other)
    def _():
        greet(d, other)

    rec = rec_ref[...]
    rec_all[d] = rec.astype(f32)
    fixed = (groups - 1) + (chips - 1) + 1
    pl.semaphore_wait(barrier, fixed + has_other.astype(jnp.int32))

    def remote(src, dst, send, recv, dp_to, tm_to):
        return pltpu.make_async_remote_copy(
            src_ref=src, dst_ref=dst, send_sem=send, recv_sem=recv,
            device_id=(dp_to, tm_to), device_id_type=MESH,
        )

    rec_copies = []
    for k in range(1, groups):
        copy = remote(rec_all.at[d], rec_all.at[d], rec_s.at[k], rec_r.at[k],
                      lax.rem(d + k, groups), i)
        copy.start()
        rec_copies.append(copy)

    mix = dot(rec, xw_ref[...]).astype(bf16)
    proj = dot(rec, bw_ref[...]).astype(bf16)
    inject, readout = proj[:, :state], proj[:, state:]
    og = og_ref[...]
    mix_t = mix.astype(f32).T
    cot_t = og.astype(f32).T
    proj_t = proj.astype(f32).T.astype(bf16)

    codes = code_ref[...].astype(f32)
    high = jnp.floor(codes * 0.125)
    low = codes - 8.0 * high
    spread = (
        lax.broadcasted_iota(jnp.int32, (heads, width), 1) // head
        == lax.broadcasted_iota(jnp.int32, (heads, width), 0)
    ).astype(f32)
    high_w, low_w = dot(high, spread), dot(low, spread)
    t_at = lax.broadcasted_iota(jnp.int32, (frames, frames), 0)
    s_at = lax.broadcasted_iota(jnp.int32, (frames, frames), 1)
    causal = t_at >= s_at
    tri = causal.astype(f32).astype(bf16)
    upper_tri = (t_at <= s_at).astype(f32).astype(bf16)
    sums = jnp.concatenate([upper_tri, jnp.ones((frames, frames), bf16)], axis=1)
    run = 8.0 * dot(tri, high_w.astype(bf16)) + dot(tri, low_w.astype(bf16))
    both = 8.0 * dot(high_w.T.astype(bf16), sums) + dot(low_w.T.astype(bf16), sums)
    run_t, total_t = both[:, :frames], both[:, frames:]
    decayed_t = jnp.exp(-unit * run_t)
    to_end_t = jnp.exp(-unit * (total_t - run_t))
    keep[...] = jnp.exp(-unit * total_t)
    mix_end = (to_end_t * mix_t).astype(bf16)
    cot_dec = (decayed_t * cot_t).astype(bf16)
    ends[...] = dot(mix_end, inject)
    starts[...] = dot(cot_dec, readout)

    part = width // CHUNKS

    def chain(first, last, target, arrive, own, sent, send_sem, recv_sem):
        for c in range(CHUNKS):
            at = pl.ds(c * part, part)
            copy = remote(sent.at[at], arrive.at[at], send_sem.at[c], recv_sem.at[c], d, target)

            @pl.when(jnp.logical_not(first))
            def _():
                copy.wait_recv()

            @pl.when(first)
            def _():
                arrive[at] = jnp.zeros((part, state), f32)

            @pl.when(jnp.logical_not(last))
            def _():
                sent[at] = keep[at] * arrive[at] + own[at]
                copy.start()

    def forward():
        chain(i == 0, i == tm - 1, lax.rem(i + 1, tm), carry, ends, sent_f, f_s, f_r)

    def backward():
        chain(i == tm - 1, i == 0, lax.rem(i + tm - 1, tm), adj, starts, sent_b, b_s, b_r)

    lower = i < tm // 2
    middle = jnp.logical_or(i == tm // 2 - 1, i == tm // 2)
    low_early = jnp.logical_and(lower, jnp.logical_not(middle))
    high_early = jnp.logical_and(jnp.logical_not(lower), jnp.logical_not(middle))
    pl.when(low_early)(forward)
    pl.when(high_early)(backward)

    scores = dot(readout, inject, 1, 1)
    cot_tb = cot_t.astype(bf16)
    pairs = jnp.zeros((frames, frames), f32)
    for h in range(heads):
        cols = slice(h * head, (h + 1) * head)
        gap = run[:, h * head:h * head + 1] - run_t[h * head:h * head + 1, :]
        decay = jnp.where(causal, jnp.exp(-unit * gap), 0.0)
        mixing = (decay * scores).astype(bf16)
        ylocal[:, cols] = dot(mixing, mix[:, cols])
        pairs = pairs + decay * dot(og[:, cols], mix[:, cols], 1, 1)
        glocal[cols, :] = dot(cot_tb[cols, :], mixing)
    pairs = pairs.astype(bf16)
    inj_local = dot(proj_t[state:], pairs)
    read_local = dot(proj_t[:state], pairs, 1, 1)

    pl.when(jnp.logical_and(lower, middle))(forward)
    pl.when(jnp.logical_not(high_early))(backward)
    pl.when(jnp.logical_not(lower))(forward)

    adj_b = adj[...].astype(bf16)
    carry_b = carry[...].astype(bf16)
    mixer_grad = to_end_t * dot(adj_b, inject, 1, 1) + glocal[...]
    inj_grad = inj_local + dot(adj_b, mix_end, 0, 0)
    read_grad = read_local + dot(carry_b, cot_dec, 0, 0)

    def rounded(a):
        return (scale * a).astype(bf16).astype(f32)

    gt[0:width] = rounded(mixer_grad)
    gt[width:width + state] = rounded(inj_grad)
    gt[width + state:width + 2 * state] = rounded(read_grad)

    g_copies = []
    for k in range(1, groups):
        to = lax.rem(d + k, groups)
        copy = remote(gt.at[pl.ds(pl.multiple_of(to * block, 8), block)], gall.at[d],
                      g_s.at[k], g_r.at[k], to, i)
        copy.start()
        g_copies.append(copy)
    gall[d] = gt[pl.ds(pl.multiple_of(d * block, 8), block)]
    y_ref[...] = (
        jnp.exp(-unit * run) * dot(readout, carry_b, 1, 1) + ylocal[...]
    ).astype(bf16)
    for copy in rec_copies:
        copy.wait_recv()
    for copy in g_copies:
        copy.wait_recv()

    lhs = jnp.concatenate([gall[r].astype(bf16) for r in range(groups)], axis=1)
    c_copies = []
    for zt in range(chips):
        rhs = jnp.concatenate(
            [rec_all[r][:, zt * 2 * rows:(zt + 1) * 2 * rows].astype(bf16) for r in range(groups)],
            axis=0,
        )
        prod = dot(lhs, rhs)
        pt[0, zt] = prod[:, :rows]
        pt[1, zt] = prod[:, rows:]
        copy = remote(pt.at[1 - core, zt], pbuf.at[zt], c_s.at[zt], c_r.at[zt], d, partner)
        copy.start()
        c_copies.append(copy)
    for copy in c_copies:
        copy.wait_recv()
    z_copies = []
    for k in range(1, chips):
        zt = lax.rem(z + k, chips)
        qs[k] = pt[core, zt] + pbuf[zt]
        copy = remote(qs.at[k], rbuf.at[k], z_s.at[k], z_r.at[k], d, zt * 2 + core)
        copy.start()
        z_copies.append(copy)
    total = pt[core, z] + pbuf[z]
    for k, copy in enumerate(z_copies, 1):
        copy.wait_recv()
        total = total + rbuf[k]
    fin[d] = total
    o_copies = []
    for k in range(1, groups):
        copy = remote(fin.at[d], fin.at[d], o_s.at[k], o_r.at[k], lax.rem(d + k, groups), i)
        copy.start()
        o_copies.append(copy)
    for copy in o_copies:
        copy.wait_recv()
    out_ref[...] = fin[...]

    for copy in rec_copies + g_copies + c_copies + z_copies + o_copies:
        copy.wait_send()

    for c in range(CHUNKS):
        at = pl.ds(c * part, part)

        @pl.when(i < tm - 1)
        def _():
            remote(sent_f.at[at], carry.at[at], f_s.at[c], f_r.at[c], d, lax.rem(i + 1, tm)).wait_send()

        @pl.when(i > 0)
        def _():
            remote(sent_b.at[at], adj.at[at], b_s.at[c], b_r.at[c], d, lax.rem(i + tm - 1, tm)).wait_send()


def body(records, x_weight, bc_weight, decay_codes, out_grad):
    signal = records[0]
    codes = decay_codes[0]
    frames, model = signal.shape
    width = x_weight.shape[1]
    wide = width + bc_weight.shape[1]
    state = bc_weight.shape[1] // 2
    tm = lax.axis_size("tm")
    groups = lax.axis_size("dp")
    chips = tm // 2
    rows = model // tm
    block = wide // groups
    grad_scale = (groups * frames * tm) ** (-0.5)
    vmem = pl.BlockSpec(memory_space=pltpu.VMEM)

    def buf(*shape):
        return pltpu.VMEM(shape, f32)

    def sems(n):
        return [pltpu.SemaphoreType.DMA((n,)), pltpu.SemaphoreType.DMA((n,))]

    y, out = pl.pallas_call(
        functools.partial(kernel, groups, tm),
        out_shape=(
            jax.ShapeDtypeStruct((frames, width), bf16),
            jax.ShapeDtypeStruct((groups, block, rows), f32),
        ),
        in_specs=[vmem] * 5,
        out_specs=(vmem, vmem),
        scratch_shapes=[
            buf(groups, frames, model),
            buf(width, state), buf(width, state), buf(width, state), buf(width, state),
            buf(width, state), buf(width, state), buf(width, state),
            buf(wide, frames), buf(groups, block, frames),
            buf(2, chips, block, rows), buf(chips, block, rows),
            buf(chips, block, rows), buf(chips, block, rows),
            buf(groups, block, rows), buf(frames, width), buf(width, frames),
            *sems(groups), *sems(CHUNKS), *sems(CHUNKS), *sems(groups),
            *sems(chips), *sems(chips), *sems(groups),
        ],
        compiler_params=pltpu.CompilerParams(
            collective_id=0, has_side_effects=True, vmem_limit_bytes=50 * 1024 * 1024
        ),
    )(signal, x_weight, bc_weight, codes, out_grad[0])
    out = out.reshape(wide, rows).T * grad_scale
    return (y[None], out[:, :width], out[:, width:])


def solution(mesh):
    return jax.shard_map(
        body,
        mesh=mesh,
        in_specs=(P("dp", "tm", None), P(), P(), P("dp", "tm", None), P("dp", "tm", None)),
        out_specs=(P("dp", "tm", None), P("tm", None), P("tm", None)),
        check_vma=False,
    )
```

time: 179 us -> 59.5 us (0.33)
  waiting for transfers between devices: 127 us -> 0 us
  Pallas kernels: 0 us -> 51.4 us
  blocking collectives: 13.5 us -> 0 us
  between operations: 14.1 us -> 0.66 us
  matrix products: 10.5 us -> 0 us
  other arithmetic: 9.79 us -> 0.03 us
  local copies, waits for them, and re-layouts: 3.76 us -> 7.11 us
    pallas_call x0 -> x1, Pallas kernels: none -> 51.4 us  [body(): pl.pallas_call(functools.partial(kernel, groups, tm), out_shape=(jax.Shap...]
    all_gather x2 -> x0, waiting for transfers between devices: 44.3 us -> none  [entering(): gathered = jax.tree.map(lambda a: lax.all_gather(a, axis), part)]
    psum x1 -> x0, waiting for transfers between devices: 44.2 us -> none  [body(): grad_share = lax.psum(grad_share, 'dp')]
    reduce_scatter x1 -> x0, waiting for transfers between devices: 38.3 us -> none  [body(): lax.psum_scatter(lax.dot_general(signal, grad_cat, (((0,), (0,)), ((), ()...]
    all_gather x1 -> x0, blocking collectives: 13.5 us -> none  [entering(): gathered = jax.tree.map(lambda a: lax.all_gather(a, axis), part)]
    dot_general x19 -> x0, matrix products: 10.5 us -> none  [the longest x1 2.2 us: body(): lax.dot_general(signal, grad_cat, (((0,), (0,)), ((), ())), preferred_ele...]
    add x7 -> x0, other arithmetic: 7.43 us -> none  [combine_pair(): later_one[0][:, :, None, None] * earlier[1] + later_one[1]]
    unnamed x12 -> x10, local copies, waits for them, and re-layouts: 2.53 us -> 5.56 us
  transfers between devices with their start and end apart: 4 -> 0, of which waited for: 4 -> 0; matrix products, arithmetic and copies ran while one was open for 3% -> 0% of each run, Pallas kernels for 0% -> 0%
where the time goes in v1:
time: 59.5 us; the launch traced here: 59.2 us
  Pallas kernels  51.4 us (86%)
  local copies, waits for them, and re-layouts  7.11 us (12%)
  between operations  0.66 us (1%)
    pallas_call x1, Pallas kernels, body(): pl.pallas_call(functools.partial(kernel, groups, tm), out_shape=(jax.Shap...  51.4 us
    unnamed x10, local copies, waits for them, and re-layouts  5.56 us
    slice x2, local copies, waits for them, and re-layouts, body(): return (y[None], out[:, :width], out[:, width:])  1.39 us

profile of v1, /device:TPU:0, one launch (start us, length us, event | category | flops | bytes accessed | tf_op | source)
XLA Modules:
  0.0 59.2 jit_solution(13257597370438518452)
XLA Ops:
  0.6 0.8 %copy.8 = s32[1,128,8]{2,1,0:T(8,128)S(1)} copy(s32[1,128,8]{1,2,0:T(8,128)} %param.8) | data formatting | bytes 8192 | tf_op args[3]
  1.4 0.0 copy-start
  1.4 1.2 %copy-done = bf16[1024,512]{1,0:T(8,128)(2,1)S(1)} copy-done((bf16[1024,512]{1,0:T(8,128)(2,1)S(1)}, bf16[1024,512]{1,0:T(8,128)(2,1)}, u32[]{:S(2)}) %copy-start) | copy-done | bytes 1048600
  2.6 0.0 copy-start.1
  2.6 1.0 %copy-done.1 = bf16[1024,256]{1,0:T(8,128)(2,1)S(1)} copy-done((bf16[1024,256]{1,0:T(8,128)(2,1)S(1)}, bf16[1024,256]{1,0:T(8,128)(2,1)}, u32[]{:S(2)}) %copy-start.1) | copy-done | bytes 524312
  3.7 0.0 copy-start.2
  3.7 0.9 %copy-done.2 = bf16[1,128,1024]{2,1,0:T(8,128)(2,1)S(1)} copy-done((bf16[1,128,1024]{2,1,0:T(8,128)(2,1)S(1)}, bf16[1,128,1024]{2,1,0:T(8,128)(2,1)}, u32[]{:S(2)}) %copy-start.2) | copy-done | bytes 262168
  4.6 0.0 copy-start.3
  4.6 0.9 %copy-done.3 = bf16[1,128,512]{2,1,0:T(8,128)(2,1)S(1)} copy-done((bf16[1,128,512]{2,1,0:T(8,128)(2,1)S(1)}, bf16[1,128,512]{2,1,0:T(8,128)(2,1)}, u32[]{:S(2)}) %copy-start.3) | copy-done | bytes 131096
  5.5 51.4 %shard_map.76 = (bf16[128,512]{1,0:T(8,128)(2,1)S(1)}, f32[4,192,128]{2,1,0:T(8,128)S(1)}) custom-call(bf16[128,1024]{1,0:T(8,128)(2,1)S(1)} %bitcast.7, bf16[1024,512]{1,0:T(8,128)(2,1)S(1)} %copy-done, bf16[1024,256]{1,0:T(8,128)(2,1)S(1)} %copy-done.1, s32[128,8]{1,0:T(8,128)S(1)} %bitcast.6, bf16[128,512]{1,0:T(8,128)(2,1)S(1)} %bitcast.8), custom_call_target="tpu_custom_call" | custom-call | tf_op jit(solution)/shard_map/pallas_call | solution.py:265
  56.9 0.2 copy.9
  57.1 0.7 %slice.9 = f32[128,256]{1,0:T(8,128)} slice(f32[128,768]{1,0:T(8,128)S(1)} %bitcast.10), slice={[0:128], [512:768]} | slice | bytes 262144 | tf_op jit(solution)/shard_map/slice | solution.py:289
  57.8 0.7 %slice.8 = f32[128,512]{1,0:T(8,128)} slice(f32[128,768]{1,0:T(8,128)S(1)} %bitcast.11), slice={[0:128], [0:512]} | slice | bytes 524288 | tf_op jit(solution)/shard_map/slice | solution.py:289
  58.5 0.7 %copy.11 = bf16[1,128,512]{2,1,0:T(8,128)(2,1)} copy(bf16[1,128,512]{2,1,0:T(8,128)(2,1)S(1)} %bitcast.9) | data formatting | bytes 262144
  (1 shorter events, 0.0 us)
Async XLA Ops:
  1.4 1.2 %copy-start = (bf16[1024,512]{1,0:T(8,128)(2,1)S(1)}, bf16[1024,512]{1,0:T(8,128)(2,1)}, u32[]{:S(2)}) copy-start(bf16[1024,512]{1,0:T(8,128)(2,1)} %xw_ref.1) | copy-start | bytes 3145732
  2.6 1.0 %copy-start.1 = (bf16[1024,256]{1,0:T(8,128)(2,1)S(1)}, bf16[1024,256]{1,0:T(8,128)(2,1)}, u32[]{:S(2)}) copy-start(bf16[1024,256]{1,0:T(8,128)(2,1)} %bw_ref.1) | copy-start | bytes 1572868
  3.7 0.9 %copy-start.2 = (bf16[1,128,1024]{2,1,0:T(8,128)(2,1)S(1)}, bf16[1,128,1024]{2,1,0:T(8,128)(2,1)}, u32[]{:S(2)}) copy-start(bf16[1,128,1024]{2,1,0:T(8,128)(2,1)} %param.5) | copy-start | bytes 786436
  4.6 0.9 %copy-start.3 = (bf16[1,128,512]{2,1,0:T(8,128)(2,1)S(1)}, bf16[1,128,512]{2,1,0:T(8,128)(2,1)}, u32[]{:S(2)}) copy-start(bf16[1,128,512]{2,1,0:T(8,128)(2,1)} %param.9) | copy-start | bytes 393220

commit v2 on v1

--- a/solution.py
+++ b/solution.py
@@ -9,6 +9,7 @@
 
 MESH = pl.DeviceIdType.MESH
 CHUNKS = 4
+PIECES = 3
 f32 = jnp.float32
 bf16 = jnp.bfloat16
 
@@ -20,20 +21,28 @@
 
 
 def kernel(
-    groups, tm, rec_ref, xw_ref, bw_ref, code_ref, og_ref, y_ref, out_ref,
-    rec_all, carry, adj, ends, starts, sent_f, sent_b, keep,
+    groups, tm, rec_hbm, xw_hbm, bw_hbm, code_hbm, og_hbm, y_ref, out_ref,
+    rec_ref, xw_ref, bw_ref, code_ref, og_ref, in_s, rec_all, rhs, carry, adj, ends, starts, sent_f, sent_b, keep,
     gt, gall, pt, pbuf, qs, rbuf, fin, ylocal, glocal,
     rec_s, rec_r, f_s, f_r, b_s, b_r, g_s, g_r, c_s, c_r, z_s, z_r, o_s, o_r,
 ):
-    frames, heads = code_ref.shape
+    heads, frames = code_ref.shape
     width = xw_ref.shape[1]
     head = width // heads
     state = bw_ref.shape[1] // 2
-    rows = out_ref.shape[2]
-    block = out_ref.shape[1]
+    piece, rows = out_ref.shape[2:]
+    block = PIECES * piece
     chips = tm // 2
     unit = 1.0 / (32.0 * frames * tm)
     scale = (state * frames * tm) ** (-0.5)
+
+    loads = []
+    for n, (src, dst) in enumerate((
+        (rec_hbm, rec_ref), (bw_hbm, bw_ref), (xw_hbm, xw_ref), (code_hbm, code_ref), (og_hbm, og_ref),
+    )):
+        load = pltpu.make_async_copy(src, dst, in_s.at[n])
+        load.start()
+        loads.append(load)
 
     d = lax.axis_index("dp")
     i = lax.axis_index("tm")
@@ -58,6 +67,7 @@
     def _():
         greet(d, other)
 
+    loads[0].wait()
     rec = rec_ref[...]
     rec_all[d] = rec.astype(f32)
     fixed = (groups - 1) + (chips - 1) + 1
@@ -76,6 +86,8 @@
         copy.start()
         rec_copies.append(copy)
 
+    for load in loads[1:]:
+        load.wait()
     mix = dot(rec, xw_ref[...]).astype(bf16)
     proj = dot(rec, bw_ref[...]).astype(bf16)
     inject, readout = proj[:, :state], proj[:, state:]
@@ -91,7 +103,8 @@
         lax.broadcasted_iota(jnp.int32, (heads, width), 1) // head
         == lax.broadcasted_iota(jnp.int32, (heads, width), 0)
     ).astype(f32)
-    high_w, low_w = dot(high, spread), dot(low, spread)
+    high_w, low_w = dot(high, spread, 0, 0), dot(low, spread, 0, 0)
+    high_t, low_t = dot(spread, high, 0, 0), dot(spread, low, 0, 0)
     t_at = lax.broadcasted_iota(jnp.int32, (frames, frames), 0)
     s_at = lax.broadcasted_iota(jnp.int32, (frames, frames), 1)
     causal = t_at >= s_at
@@ -99,7 +112,7 @@
     upper_tri = (t_at <= s_at).astype(f32).astype(bf16)
     sums = jnp.concatenate([upper_tri, jnp.ones((frames, frames), bf16)], axis=1)
     run = 8.0 * dot(tri, high_w.astype(bf16)) + dot(tri, low_w.astype(bf16))
-    both = 8.0 * dot(high_w.T.astype(bf16), sums) + dot(low_w.T.astype(bf16), sums)
+    both = 8.0 * dot(high_t.astype(bf16), sums) + dot(low_t.astype(bf16), sums)
     run_t, total_t = both[:, :frames], both[:, frames:]
     decayed_t = jnp.exp(-unit * run_t)
     to_end_t = jnp.exp(-unit * (total_t - run_t))
@@ -175,53 +188,64 @@
     gt[width + state:width + 2 * state] = rounded(read_grad)
 
     g_copies = []
-    for k in range(1, groups):
-        to = lax.rem(d + k, groups)
-        copy = remote(gt.at[pl.ds(pl.multiple_of(to * block, 8), block)], gall.at[d],
-                      g_s.at[k], g_r.at[k], to, i)
-        copy.start()
-        g_copies.append(copy)
-    gall[d] = gt[pl.ds(pl.multiple_of(d * block, 8), block)]
+    for q in range(PIECES):
+        for k in range(1, groups):
+            to = lax.rem(d + k, groups)
+            at = pl.ds(pl.multiple_of(to * block + q * piece, 8), piece)
+            copy = remote(gt.at[at], gall.at[d, q], g_s.at[q, k], g_r.at[q, k], to, i)
+            copy.start()
+            g_copies.append(copy)
+        gall[d, q] = gt[pl.ds(pl.multiple_of(d * block + q * piece, 8), piece)]
     y_ref[...] = (
         jnp.exp(-unit * run) * dot(readout, carry_b, 1, 1) + ylocal[...]
     ).astype(bf16)
     for copy in rec_copies:
         copy.wait_recv()
-    for copy in g_copies:
-        copy.wait_recv()
-
-    lhs = jnp.concatenate([gall[r].astype(bf16) for r in range(groups)], axis=1)
-    c_copies = []
-    for zt in range(chips):
-        rhs = jnp.concatenate(
-            [rec_all[r][:, zt * 2 * rows:(zt + 1) * 2 * rows].astype(bf16) for r in range(groups)],
-            axis=0,
-        )
-        prod = dot(lhs, rhs)
-        pt[0, zt] = prod[:, :rows]
-        pt[1, zt] = prod[:, rows:]
-        copy = remote(pt.at[1 - core, zt], pbuf.at[zt], c_s.at[zt], c_r.at[zt], d, partner)
+    for r in range(groups):
+        rhs[r * frames:(r + 1) * frames] = rec_all[r].astype(bf16)
+
+    c_copies, z_copies, o_copies = [], [], []
+
+    def product(q):
+        for copy in g_copies[q * (groups - 1):(q + 1) * (groups - 1)]:
+            copy.wait_recv()
+        lhs = jnp.concatenate([gall[r, q].astype(bf16) for r in range(groups)], axis=1)
+        for zt in range(chips):
+            prod = dot(lhs, rhs[:, zt * 2 * rows:(zt + 1) * 2 * rows])
+            pt[0, q, zt] = prod[:, :rows]
+            pt[1, q, zt] = prod[:, rows:]
+        copy = remote(pt.at[1 - core, q], pbuf.at[q], c_s.at[q], c_r.at[q], d, partner)
         copy.start()
         c_copies.append(copy)
-    for copy in c_copies:
-        copy.wait_recv()
-    z_copies = []
-    for k in range(1, chips):
-        zt = lax.rem(z + k, chips)
-        qs[k] = pt[core, zt] + pbuf[zt]
-        copy = remote(qs.at[k], rbuf.at[k], z_s.at[k], z_r.at[k], d, zt * 2 + core)
-        copy.start()
-        z_copies.append(copy)
-    total = pt[core, z] + pbuf[z]
-    for k, copy in enumerate(z_copies, 1):
-        copy.wait_recv()
-        total = total + rbuf[k]
-    fin[d] = total
-    o_copies = []
-    for k in range(1, groups):
-        copy = remote(fin.at[d], fin.at[d], o_s.at[k], o_r.at[k], lax.rem(d + k, groups), i)
-        copy.start()
-        o_copies.append(copy)
+
+    def over_chips(q):
+        c_copies[q].wait_recv()
+        for k in range(1, chips):
+            zt = lax.rem(z + k, chips)
+            qs[q, k] = pt[core, q, zt] + pbuf[q, zt]
+            copy = remote(qs.at[q, k], rbuf.at[q, k], z_s.at[q, k], z_r.at[q, k], d, zt * 2 + core)
+            copy.start()
+            z_copies.append(copy)
+
+    def over_groups(q):
+        total = pt[core, q, z] + pbuf[q, z]
+        for k in range(1, chips):
+            z_copies[q * (chips - 1) + k - 1].wait_recv()
+            total = total + rbuf[q, k]
+        fin[d, q] = total
+        for k in range(1, groups):
+            copy = remote(fin.at[d, q], fin.at[d, q], o_s.at[q, k], o_r.at[q, k],
+                          lax.rem(d + k, groups), i)
+            copy.start()
+            o_copies.append(copy)
+
+    for step in range(PIECES + 2):
+        if step < PIECES:
+            product(step)
+        if 1 <= step <= PIECES:
+            over_chips(step - 1)
+        if step >= 2:
+            over_groups(step - 2)
     for copy in o_copies:
         copy.wait_recv()
     out_ref[...] = fin[...]
@@ -243,7 +267,7 @@
 
 def body(records, x_weight, bc_weight, decay_codes, out_grad):
     signal = records[0]
-    codes = decay_codes[0]
+    codes = decay_codes[0].T
     frames, model = signal.shape
     width = x_weight.shape[1]
     wide = width + bc_weight.shape[1]
@@ -252,37 +276,40 @@
     groups = lax.axis_size("dp")
     chips = tm // 2
     rows = model // tm
-    block = wide // groups
+    piece = wide // groups // PIECES
     grad_scale = (groups * frames * tm) ** (-0.5)
     vmem = pl.BlockSpec(memory_space=pltpu.VMEM)
 
     def buf(*shape):
         return pltpu.VMEM(shape, f32)
 
-    def sems(n):
-        return [pltpu.SemaphoreType.DMA((n,)), pltpu.SemaphoreType.DMA((n,))]
+    def sems(*n):
+        return [pltpu.SemaphoreType.DMA(n), pltpu.SemaphoreType.DMA(n)]
 
     y, out = pl.pallas_call(
         functools.partial(kernel, groups, tm),
         out_shape=(
             jax.ShapeDtypeStruct((frames, width), bf16),
-            jax.ShapeDtypeStruct((groups, block, rows), f32),
+            jax.ShapeDtypeStruct((groups, PIECES, piece, rows), f32),
         ),
-        in_specs=[vmem] * 5,
+        in_specs=[pl.BlockSpec(memory_space=pl.ANY)] * 5,
         out_specs=(vmem, vmem),
         scratch_shapes=[
-            buf(groups, frames, model),
+            pltpu.VMEM((frames, model), bf16), pltpu.VMEM(x_weight.shape, bf16),
+            pltpu.VMEM(bc_weight.shape, bf16), pltpu.VMEM(codes.shape, jnp.int32),
+            pltpu.VMEM((frames, width), bf16), pltpu.SemaphoreType.DMA((5,)),
+            buf(groups, frames, model), pltpu.VMEM((groups * frames, model), bf16),
             buf(width, state), buf(width, state), buf(width, state), buf(width, state),
             buf(width, state), buf(width, state), buf(width, state),
-            buf(wide, frames), buf(groups, block, frames),
-            buf(2, chips, block, rows), buf(chips, block, rows),
-            buf(chips, block, rows), buf(chips, block, rows),
-            buf(groups, block, rows), buf(frames, width), buf(width, frames),
-            *sems(groups), *sems(CHUNKS), *sems(CHUNKS), *sems(groups),
-            *sems(chips), *sems(chips), *sems(groups),
+            buf(wide, frames), buf(groups, PIECES, piece, frames),
+            buf(2, PIECES, chips, piece, rows), buf(PIECES, chips, piece, rows),
+            buf(PIECES, chips, piece, rows), buf(PIECES, chips, piece, rows),
+            buf(groups, PIECES, piece, rows), buf(frames, width), buf(width, frames),
+            *sems(groups), *sems(CHUNKS), *sems(CHUNKS), *sems(PIECES, groups),
+            *sems(PIECES), *sems(PIECES, chips), *sems(PIECES, groups),
         ],
         compiler_params=pltpu.CompilerParams(
-            collective_id=0, has_side_effects=True, vmem_limit_bytes=50 * 1024 * 1024
+            collective_id=0, has_side_effects=True, vmem_limit_bytes=60 * 1024 * 1024
         ),
     )(signal, x_weight, bc_weight, codes, out_grad[0])
     out = out.reshape(wide, rows).T * grad_scale

time: 59.5 us -> 53.5 us (0.90)
  local copies, waits for them, and re-layouts: 7.11 us -> 2.43 us
  Pallas kernels: 51.4 us -> 49.2 us
  other arithmetic: 0.03 us -> 1.02 us
    unnamed x10 -> x3, local copies, waits for them, and re-layouts: 5.56 us -> 0.88 us
    pallas_call x1, Pallas kernels: 51.4 us -> 49.2 us  [body(): pl.pallas_call(functools.partial(kernel, groups, tm), out_shape=(jax.Shap...]
    mul x1, other arithmetic: 0.03 us -> 1.02 us  [body(): out = out.reshape(wide, rows).T * grad_scale]
where the time goes in v2:
time: 53.5 us; the launch traced here: 53.3 us
  Pallas kernels  49.2 us (92%)
  local copies, waits for them, and re-layouts  2.43 us (5%)
  other arithmetic  1.02 us (2%)
  between operations  0.66 us (1%)
    pallas_call x1, Pallas kernels, body(): pl.pallas_call(functools.partial(kernel, groups, tm), out_shape=(jax.Shap...  49.2 us
    slice x2, local copies, waits for them, and re-layouts, body(): return (y[None], out[:, :width], out[:, width:])  1.39 us

profile of v2, /device:TPU:0, one launch (start us, length us, event | category | flops | bytes accessed | tf_op | source)
XLA Modules:
  0.0 53.3 jit_solution(9401290216076774905)
XLA Ops:
  0.6 49.2 %shard_map.76 = (bf16[128,512]{1,0:T(8,128)(2,1)}, f32[4,3,64,128]{3,2,1,0:T(8,128)}) custom-call(bf16[128,1024]{1,0:T(8,128)(2,1)} %bitcast.11, bf16[1024,512]{1,0:T(8,128)(2,1)} %xw_hbm.1, bf16[1024,256]{1,0:T(8,128)(2,1)} %bw_hbm.1, s32[8,128]{1,0:T(8,128)} %bitcast.14, bf16[128,512]{1,0:T(8,128)(2,1)} %bitcast.13), custom_call_target="tpu_custom_call" | custom-call | tf_op jit(solution)/shard_map/pallas_call | solution.py:289
  49.9 1.0 %broadcast_multiply_fusion = f32[4,3,64,128]{3,2,1,0:T(8,128)S(1)} fusion(f32[4,3,64,128]{3,2,1,0:T(8,128)} %get-tuple-element.6), kind=kLoop, calls=%fused_computation | loop fusion | flops 98304 | bytes 786432 | tf_op jit(solution)/shard_map/mul | solution.py:315
  50.9 0.2 copy.8
  51.1 0.7 %slice.9 = f32[128,256]{1,0:T(8,128)} slice(f32[128,768]{1,0:T(8,128)S(1)} %bitcast.8), slice={[0:128], [512:768]} | slice | bytes 262144 | tf_op jit(solution)/shard_map/slice | solution.py:316
  51.7 0.0 copy-start
  51.7 0.7 %slice.8 = f32[128,512]{1,0:T(8,128)} slice(f32[128,768]{1,0:T(8,128)S(1)} %bitcast.9), slice={[0:128], [0:512]} | slice | bytes 524288 | tf_op jit(solution)/shard_map/slice | solution.py:316
  52.5 0.2 copy-done
  52.7 0.7 %copy.10 = bf16[1,128,512]{2,1,0:T(8,128)(2,1)} copy(bf16[1,128,512]{2,1,0:T(8,128)(2,1)S(1)} %bitcast.12) | data formatting | bytes 262144
Async XLA Ops:
  51.7 1.0 %copy-start = (bf16[128,512]{1,0:T(8,128)(2,1)S(1)}, bf16[128,512]{1,0:T(8,128)(2,1)}, u32[]{:S(2)}) copy-start(bf16[128,512]{1,0:T(8,128)(2,1)} %get-tuple-element.5) | copy-start | bytes 393220

commit v3 on v2

--- a/solution.py
+++ b/solution.py
@@ -21,16 +21,16 @@
 
 
 def kernel(
-    groups, tm, rec_hbm, xw_hbm, bw_hbm, code_hbm, og_hbm, y_ref, out_ref,
-    rec_ref, xw_ref, bw_ref, code_ref, og_ref, in_s, rec_all, rhs, carry, adj, ends, starts, sent_f, sent_b, keep,
+    groups, tm, rec_hbm, xw_hbm, bw_hbm, code_hbm, og_hbm, y_ref, x_out, bc_out,
+    rec_ref, xw_ref, bw_ref, code_ref, og_ref, in_s, rec_all, rhs, own, give, given, give_d, given_d, hop_in, hop_out, entering, passed,
     gt, gall, pt, pbuf, qs, rbuf, fin, ylocal, glocal,
-    rec_s, rec_r, f_s, f_r, b_s, b_r, g_s, g_r, c_s, c_r, z_s, z_r, o_s, o_r,
+    rec_s, rec_r, e_s, e_r, h_s, h_r, p_s, p_r, g_s, g_r, c_s, c_r, z_s, z_r, o_s, o_r,
 ):
     heads, frames = code_ref.shape
     width = xw_ref.shape[1]
     head = width // heads
     state = bw_ref.shape[1] // 2
-    piece, rows = out_ref.shape[2:]
+    piece, rows = fin.shape[2:]
     block = PIECES * piece
     chips = tm // 2
     unit = 1.0 / (32.0 * frames * tm)
@@ -49,8 +49,6 @@
     z = i // 2
     core = i % 2
     partner = i + 1 - 2 * core
-    other = i - 1 + 2 * core
-    has_other = jnp.logical_and(other >= 0, other < tm)
 
     barrier = pltpu.get_barrier_semaphore()
 
@@ -63,15 +61,10 @@
         greet(d, lax.rem(z + k, chips) * 2 + core)
     greet(d, partner)
 
-    @pl.when(has_other)
-    def _():
-        greet(d, other)
-
     loads[0].wait()
     rec = rec_ref[...]
     rec_all[d] = rec.astype(f32)
-    fixed = (groups - 1) + (chips - 1) + 1
-    pl.semaphore_wait(barrier, fixed + has_other.astype(jnp.int32))
+    pl.semaphore_wait(barrier, (groups - 1) + (chips - 1) + 1)
 
     def remote(src, dst, send, recv, dp_to, tm_to):
         return pltpu.make_async_remote_copy(
@@ -80,11 +73,26 @@
         )
 
     rec_copies = []
-    for k in range(1, groups):
-        copy = remote(rec_all.at[d], rec_all.at[d], rec_s.at[k], rec_r.at[k],
-                      lax.rem(d + k, groups), i)
+
+    def send_rec(n, source, half, to):
+        size = frames if half is None else frames // 2
+        ref = rec_all.at[source, pl.ds((half or 0) * size, size)]
+        copy = remote(ref, ref, rec_s.at[n], rec_r.at[n], to, i)
         copy.start()
         rec_copies.append(copy)
+        return copy
+
+    square = groups == 4
+    if square:
+        beside = d + 1 - 2 * (d % 2)
+        across = lax.rem(d + 2, groups)
+        first_a = send_rec(0, d, 0, beside)
+        first_b = send_rec(1, d, 1, across)
+        send_rec(2, d, 1, beside)
+        send_rec(3, d, 0, across)
+    else:
+        for k in range(1, groups):
+            send_rec(k, d, None, lax.rem(d + k, groups))
 
     for load in loads[1:]:
         load.wait()
@@ -116,44 +124,72 @@
     run_t, total_t = both[:, :frames], both[:, frames:]
     decayed_t = jnp.exp(-unit * run_t)
     to_end_t = jnp.exp(-unit * (total_t - run_t))
-    keep[...] = jnp.exp(-unit * total_t)
     mix_end = (to_end_t * mix_t).astype(bf16)
     cot_dec = (decayed_t * cot_t).astype(bf16)
-    ends[...] = dot(mix_end, inject)
-    starts[...] = dot(cot_dec, readout)
+    ones = jnp.ones((frames, 128), f32)
+    give_d[...] = jnp.exp(-unit * (8.0 * dot(high, ones) + dot(low, ones)))
+    ends = dot(mix_end, inject)
+    starts = dot(cot_dec, readout)
+
+    forward = core == 1
+
+    @pl.when(forward)
+    def _():
+        own[...] = ends
+        give[...] = starts
+
+    @pl.when(jnp.logical_not(forward))
+    def _():
+        own[...] = starts
+        give[...] = ends
 
     part = width // CHUNKS
-
-    def chain(first, last, target, arrive, own, sent, send_sem, recv_sem):
+    per = heads // CHUNKS
+    place = jnp.where(forward, z, chips - 1 - z)
+    onward = lax.rem(jnp.where(forward, z + 1, z + chips - 1), chips) * 2 + core
+    exchange = [remote(give_d, given_d, e_s.at[CHUNKS], e_r.at[CHUNKS], d, partner)]
+    hops, passes = [], []
+    for c in range(CHUNKS):
+        at = pl.ds(c * part, part)
+        exchange.append(remote(give.at[at], given.at[at], e_s.at[c], e_r.at[c], d, partner))
+        hops.append(remote(hop_out.at[at], hop_in.at[at], h_s.at[c], h_r.at[c], d, onward))
+        passes.append(remote(hop_in.at[at], passed.at[at], p_s.at[c], p_r.at[c], d, partner))
+    for copy in exchange:
+        copy.start()
+
+    def chain():
+        exchange[0].wait_recv()
+
+        def factors(ref, c):
+            return jnp.concatenate(
+                [jnp.broadcast_to(ref[h:h + 1, :], (head, 128)) for h in range(c * per, (c + 1) * per)],
+                axis=0,
+            )
+
         for c in range(CHUNKS):
             at = pl.ds(c * part, part)
-            copy = remote(sent.at[at], arrive.at[at], send_sem.at[c], recv_sem.at[c], d, target)
-
-            @pl.when(jnp.logical_not(first))
+            exchange[c + 1].wait_recv()
+
+            @pl.when(place > 0)
             def _():
-                copy.wait_recv()
-
-            @pl.when(first)
+                hops[c].wait_recv()
+
+            @pl.when(place == 0)
             def _():
-                arrive[at] = jnp.zeros((part, state), f32)
-
-            @pl.when(jnp.logical_not(last))
+                hop_in[at] = jnp.zeros((part, state), f32)
+
+            inside = factors(given_d, c) * hop_in[at] + given[at]
+            entering[at] = inside
+
+            @pl.when(place < chips - 1)
             def _():
-                sent[at] = keep[at] * arrive[at] + own[at]
-                copy.start()
-
-    def forward():
-        chain(i == 0, i == tm - 1, lax.rem(i + 1, tm), carry, ends, sent_f, f_s, f_r)
-
-    def backward():
-        chain(i == tm - 1, i == 0, lax.rem(i + tm - 1, tm), adj, starts, sent_b, b_s, b_r)
-
-    lower = i < tm // 2
-    middle = jnp.logical_or(i == tm // 2 - 1, i == tm // 2)
-    low_early = jnp.logical_and(lower, jnp.logical_not(middle))
-    high_early = jnp.logical_and(jnp.logical_not(lower), jnp.logical_not(middle))
-    pl.when(low_early)(forward)
-    pl.when(high_early)(backward)
+                hop_out[at] = factors(give_d, c) * inside + own[at]
+                hops[c].start()
+
+            passes[c].start()
+
+    early = place < chips // 2
+    pl.when(early)(chain)
 
     scores = dot(readout, inject, 1, 1)
     cot_tb = cot_t.astype(bf16)
@@ -170,12 +206,19 @@
     inj_local = dot(proj_t[state:], pairs)
     read_local = dot(proj_t[:state], pairs, 1, 1)
 
-    pl.when(jnp.logical_and(lower, middle))(forward)
-    pl.when(jnp.logical_not(high_early))(backward)
-    pl.when(jnp.logical_not(lower))(forward)
-
-    adj_b = adj[...].astype(bf16)
-    carry_b = carry[...].astype(bf16)
+    if square:
+        first_a.wait_recv()
+        send_rec(4, beside, 0, across)
+        first_b.wait_recv()
+        send_rec(5, across, 1, beside)
+
+    pl.when(jnp.logical_not(early))(chain)
+    for copy in passes:
+        copy.wait_recv()
+
+    mine, theirs = entering[...].astype(bf16), passed[...].astype(bf16)
+    carry_b = jnp.where(forward, mine, theirs)
+    adj_b = jnp.where(forward, theirs, mine)
     mixer_grad = to_end_t * dot(adj_b, inject, 1, 1) + glocal[...]
     inj_grad = inj_local + dot(adj_b, mix_end, 0, 0)
     read_grad = read_local + dot(carry_b, cot_dec, 0, 0)
@@ -200,7 +243,8 @@
         jnp.exp(-unit * run) * dot(readout, carry_b, 1, 1) + ylocal[...]
     ).astype(bf16)
     for copy in rec_copies:
-        copy.wait_recv()
+        if not (square and (copy is first_a or copy is first_b)):
+            copy.wait_recv()
     for r in range(groups):
         rhs[r * frames:(r + 1) * frames] = rec_all[r].astype(bf16)
 
@@ -248,21 +292,14 @@
             over_groups(step - 2)
     for copy in o_copies:
         copy.wait_recv()
-    out_ref[...] = fin[...]
-
-    for copy in rec_copies + g_copies + c_copies + z_copies + o_copies:
+    whole = fin[...].reshape(groups * block, rows).T * ((groups * frames * tm) ** (-0.5))
+    x_out[...] = whole[:, :width]
+    bc_out[...] = whole[:, width:]
+
+    for copy in rec_copies + exchange + passes + g_copies + c_copies + z_copies + o_copies:
         copy.wait_send()
-
-    for c in range(CHUNKS):
-        at = pl.ds(c * part, part)
-
-        @pl.when(i < tm - 1)
-        def _():
-            remote(sent_f.at[at], carry.at[at], f_s.at[c], f_r.at[c], d, lax.rem(i + 1, tm)).wait_send()
-
-        @pl.when(i > 0)
-        def _():
-            remote(sent_b.at[at], adj.at[at], b_s.at[c], b_r.at[c], d, lax.rem(i + tm - 1, tm)).wait_send()
+    for copy in hops:
+        pl.when(place < chips - 1)(copy.wait_send)
 
 
 def body(records, x_weight, bc_weight, decay_codes, out_grad):
@@ -277,7 +314,6 @@
     chips = tm // 2
     rows = model // tm
     piece = wide // groups // PIECES
-    grad_scale = (groups * frames * tm) ** (-0.5)
     vmem = pl.BlockSpec(memory_space=pltpu.VMEM)
 
     def buf(*shape):
@@ -286,34 +322,35 @@
     def sems(*n):
         return [pltpu.SemaphoreType.DMA(n), pltpu.SemaphoreType.DMA(n)]
 
-    y, out = pl.pallas_call(
+    y, x_grad, bc_grad = pl.pallas_call(
         functools.partial(kernel, groups, tm),
         out_shape=(
             jax.ShapeDtypeStruct((frames, width), bf16),
-            jax.ShapeDtypeStruct((groups, PIECES, piece, rows), f32),
+            jax.ShapeDtypeStruct((rows, width), f32),
+            jax.ShapeDtypeStruct((rows, wide - width), f32),
         ),
         in_specs=[pl.BlockSpec(memory_space=pl.ANY)] * 5,
-        out_specs=(vmem, vmem),
+        out_specs=(vmem, vmem, vmem),
         scratch_shapes=[
             pltpu.VMEM((frames, model), bf16), pltpu.VMEM(x_weight.shape, bf16),
             pltpu.VMEM(bc_weight.shape, bf16), pltpu.VMEM(codes.shape, jnp.int32),
             pltpu.VMEM((frames, width), bf16), pltpu.SemaphoreType.DMA((5,)),
             buf(groups, frames, model), pltpu.VMEM((groups * frames, model), bf16),
+            buf(width, state), buf(width, state), buf(width, state),
+            buf(codes.shape[0], 128), buf(codes.shape[0], 128),
             buf(width, state), buf(width, state), buf(width, state), buf(width, state),
-            buf(width, state), buf(width, state), buf(width, state),
             buf(wide, frames), buf(groups, PIECES, piece, frames),
             buf(2, PIECES, chips, piece, rows), buf(PIECES, chips, piece, rows),
             buf(PIECES, chips, piece, rows), buf(PIECES, chips, piece, rows),
             buf(groups, PIECES, piece, rows), buf(frames, width), buf(width, frames),
-            *sems(groups), *sems(CHUNKS), *sems(CHUNKS), *sems(PIECES, groups),
+            *sems(max(groups, 6)), *sems(CHUNKS + 1), *sems(CHUNKS), *sems(CHUNKS), *sems(PIECES, groups),
             *sems(PIECES), *sems(PIECES, chips), *sems(PIECES, groups),
         ],
         compiler_params=pltpu.CompilerParams(
             collective_id=0, has_side_effects=True, vmem_limit_bytes=60 * 1024 * 1024
         ),
     )(signal, x_weight, bc_weight, codes, out_grad[0])
-    out = out.reshape(wide, rows).T * grad_scale
-    return (y[None], out[:, :width], out[:, width:])
+    return (y[None], x_grad, bc_grad)
 
 
 def solution(mesh):

time: 53.5 us -> 47.9 us (0.90)
  Pallas kernels: 49.2 us -> 43.8 us
  other arithmetic: 1.02 us -> 0 us
  local copies, waits for them, and re-layouts: 2.43 us -> 3.27 us
    pallas_call x1, Pallas kernels: 49.2 us -> 43.8 us  [body(): pl.pallas_call(functools.partial(kernel, groups, tm), out_shape=(jax.Shap...]
    unnamed x3 -> x7, local copies, waits for them, and re-layouts: 0.88 us -> 3.27 us
    slice x2 -> x0, local copies, waits for them, and re-layouts: 1.39 us -> none  [body(): return (y[None], out[:, :width], out[:, width:])]
    mul x1 -> x0, other arithmetic: 1.02 us -> none  [body(): out = out.reshape(wide, rows).T * grad_scale]
where the time goes in v3:
time: 47.9 us; the launch traced here: 47.7 us
  Pallas kernels  43.8 us (91%)
  local copies, waits for them, and re-layouts  3.27 us (7%)
  between operations  0.65 us (1%)
    pallas_call x1, Pallas kernels, body(): pl.pallas_call(functools.partial(kernel, groups, tm), out_shape=(jax.Shap...  43.8 us
    unnamed x7, local copies, waits for them, and re-layouts  3.27 us

profile of v3, /device:TPU:0, one launch (start us, length us, event | category | flops | bytes accessed | tf_op | source)
XLA Modules:
  0.0 47.7 jit_solution(416639283312677305)
XLA Ops:
  0.6 43.8 %shard_map.76 = (bf16[128,512]{1,0:T(8,128)(2,1)}, f32[128,512]{1,0:T(8,128)}, f32[128,256]{1,0:T(8,128)}) custom-call(bf16[128,1024]{1,0:T(8,128)(2,1)} %bitcast.6, bf16[1024,512]{1,0:T(8,128)(2,1)} %xw_hbm.1, bf16[1024,256]{1,0:T(8,128)(2,1)} %bw_hbm.1, s32[8,128]{1,0:T(8,128)} %bitcast.9, bf16[128,512]{1,0:T(8,128)(2,1)} %bitcast.8), custom_call_target="tpu_custom_call" | custom-call | tf_op jit(solution)/shard_map/pallas_call | solution.py:325
  44.4 0.0 copy-start
  44.5 1.6 %copy.11 = bf16[1,128,512]{2,1,0:T(8,128)(2,1)} copy(bf16[1,128,512]{2,1,0:T(8,128)(2,1)} %bitcast.7) | data formatting | bytes 262144
  46.1 0.0 copy-done
  46.1 0.0 copy-start.1
  46.1 0.7 %copy.12 = f32[128,512]{1,0:T(8,128)} copy(f32[128,512]{1,0:T(8,128)S(1)} %copy-done) | data formatting | bytes 524288
  46.8 0.3 copy-done.1
  47.1 0.7 %copy.13 = f32[128,256]{1,0:T(8,128)} copy(f32[128,256]{1,0:T(8,128)S(1)} %copy-done.1) | data formatting | bytes 262144
Async XLA Ops:
  44.4 1.6 %copy-start = (f32[128,512]{1,0:T(8,128)S(1)}, f32[128,512]{1,0:T(8,128)}, u32[]{:S(2)}) copy-start(f32[128,512]{1,0:T(8,128)} %get-tuple-element.13) | copy-start | bytes 786436
  46.1 1.0 %copy-start.1 = (f32[128,256]{1,0:T(8,128)S(1)}, f32[128,256]{1,0:T(8,128)}, u32[]{:S(2)}) copy-start(f32[128,256]{1,0:T(8,128)} %get-tuple-element.14) | copy-start | bytes 393220

commit v4 on v3

--- a/solution.py
+++ b/solution.py
@@ -8,7 +8,7 @@
 from jax.sharding import PartitionSpec as P
 
 MESH = pl.DeviceIdType.MESH
-CHUNKS = 4
+CHUNKS = 8
 PIECES = 3
 f32 = jnp.float32
 bf16 = jnp.bfloat16
@@ -74,11 +74,12 @@
 
     rec_copies = []
 
-    def send_rec(n, source, half, to):
+    def send_rec(n, source, half, to, start=True):
         size = frames if half is None else frames // 2
         ref = rec_all.at[source, pl.ds((half or 0) * size, size)]
         copy = remote(ref, ref, rec_s.at[n], rec_r.at[n], to, i)
-        copy.start()
+        if start:
+            copy.start()
         rec_copies.append(copy)
         return copy
 
@@ -90,6 +91,8 @@
         first_b = send_rec(1, d, 1, across)
         send_rec(2, d, 1, beside)
         send_rec(3, d, 0, across)
+        relay_a = send_rec(4, beside, 0, across, False)
+        relay_b = send_rec(5, across, 1, beside, False)
     else:
         for k in range(1, groups):
             send_rec(k, d, None, lax.rem(d + k, groups))
@@ -157,8 +160,9 @@
     for copy in exchange:
         copy.start()
 
-    def chain():
-        exchange[0].wait_recv()
+    def chain(chunks):
+        if chunks[0] == 0:
+            exchange[0].wait_recv()
 
         def factors(ref, c):
             return jnp.concatenate(
@@ -166,7 +170,7 @@
                 axis=0,
             )
 
-        for c in range(CHUNKS):
+        for c in chunks:
             at = pl.ds(c * part, part)
             exchange[c + 1].wait_recv()
 
@@ -189,7 +193,19 @@
             passes[c].start()
 
     early = place < chips // 2
-    pl.when(early)(chain)
+    late = jnp.logical_not(early)
+
+    def relay():
+        if square:
+            first_a.wait_recv()
+            relay_a.start()
+            first_b.wait_recv()
+            relay_b.start()
+
+    @pl.when(early)
+    def _():
+        chain(range(CHUNKS))
+        relay()
 
     scores = dot(readout, inject, 1, 1)
     cot_tb = cot_t.astype(bf16)
@@ -206,39 +222,42 @@
     inj_local = dot(proj_t[state:], pairs)
     read_local = dot(proj_t[:state], pairs, 1, 1)
 
-    if square:
-        first_a.wait_recv()
-        send_rec(4, beside, 0, across)
-        first_b.wait_recv()
-        send_rec(5, across, 1, beside)
-
-    pl.when(jnp.logical_not(early))(chain)
-    for copy in passes:
-        copy.wait_recv()
-
-    mine, theirs = entering[...].astype(bf16), passed[...].astype(bf16)
-    carry_b = jnp.where(forward, mine, theirs)
-    adj_b = jnp.where(forward, theirs, mine)
-    mixer_grad = to_end_t * dot(adj_b, inject, 1, 1) + glocal[...]
-    inj_grad = inj_local + dot(adj_b, mix_end, 0, 0)
-    read_grad = read_local + dot(carry_b, cot_dec, 0, 0)
+    pl.when(late)(relay)
 
     def rounded(a):
         return (scale * a).astype(bf16).astype(f32)
 
-    gt[0:width] = rounded(mixer_grad)
-    gt[width:width + state] = rounded(inj_grad)
-    gt[width + state:width + 2 * state] = rounded(read_grad)
-
     g_copies = []
-    for q in range(PIECES):
+
+    def send_g(q):
         for k in range(1, groups):
             to = lax.rem(d + k, groups)
-            at = pl.ds(pl.multiple_of(to * block + q * piece, 8), piece)
+            at = pl.ds(pl.multiple_of((q * groups + to) * piece, 8), piece)
             copy = remote(gt.at[at], gall.at[d, q], g_s.at[q, k], g_r.at[q, k], to, i)
             copy.start()
             g_copies.append(copy)
-        gall[d, q] = gt[pl.ds(pl.multiple_of(d * block + q * piece, 8), piece)]
+        gall[d, q] = gt[pl.ds(pl.multiple_of((q * groups + d) * piece, 8), piece)]
+
+    split = groups * piece
+    adjs, carries = [], []
+    for q in range(PIECES - 1):
+        at = slice(q * split, (q + 1) * split)
+        chunks = range(q * split // part, (q + 1) * split // part)
+        pl.when(late)(functools.partial(chain, chunks))
+        for c in chunks:
+            passes[c].wait_recv()
+        mine, theirs = entering[at].astype(bf16), passed[at].astype(bf16)
+        adjs.append(jnp.where(forward, theirs, mine))
+        carries.append(jnp.where(forward, mine, theirs))
+        gt[at] = rounded(to_end_t[at] * dot(adjs[q], inject, 1, 1) + glocal[at])
+        send_g(q)
+    adj_b = jnp.concatenate(adjs, axis=0)
+    carry_b = jnp.concatenate(carries, axis=0)
+    inj_grad = inj_local + dot(adj_b, mix_end, 0, 0)
+    read_grad = read_local + dot(carry_b, cot_dec, 0, 0)
+    gt[width:width + state] = rounded(inj_grad)
+    gt[width + state:width + 2 * state] = rounded(read_grad)
+    send_g(PIECES - 1)
     y_ref[...] = (
         jnp.exp(-unit * run) * dot(readout, carry_b, 1, 1) + ylocal[...]
     ).astype(bf16)
@@ -276,9 +295,9 @@
         for k in range(1, chips):
             z_copies[q * (chips - 1) + k - 1].wait_recv()
             total = total + rbuf[q, k]
-        fin[d, q] = total
+        fin[q, d] = total
         for k in range(1, groups):
-            copy = remote(fin.at[d, q], fin.at[d, q], o_s.at[q, k], o_r.at[q, k],
+            copy = remote(fin.at[q, d], fin.at[q, d], o_s.at[q, k], o_r.at[q, k],
                           lax.rem(d + k, groups), i)
             copy.start()
             o_copies.append(copy)
@@ -325,11 +344,11 @@
     y, x_grad, bc_grad = pl.pallas_call(
         functools.partial(kernel, groups, tm),
         out_shape=(
-            jax.ShapeDtypeStruct((frames, width), bf16),
-            jax.ShapeDtypeStruct((rows, width), f32),
-            jax.ShapeDtypeStruct((rows, wide - width), f32),
+            pltpu.VMEM((frames, width), bf16),
+            pltpu.VMEM((rows, width), f32),
+            pltpu.VMEM((rows, wide - width), f32),
         ),
-        in_specs=[pl.BlockSpec(memory_space=pl.ANY)] * 5,
+        in_specs=[pl.BlockSpec(memory_space=pltpu.HBM)] * 5,
         out_specs=(vmem, vmem, vmem),
         scratch_shapes=[
             pltpu.VMEM((frames, model), bf16), pltpu.VMEM(x_weight.shape, bf16),
@@ -342,7 +361,7 @@
             buf(wide, frames), buf(groups, PIECES, piece, frames),
             buf(2, PIECES, chips, piece, rows), buf(PIECES, chips, piece, rows),
             buf(PIECES, chips, piece, rows), buf(PIECES, chips, piece, rows),
-            buf(groups, PIECES, piece, rows), buf(frames, width), buf(width, frames),
+            buf(PIECES, groups, piece, rows), buf(frames, width), buf(width, frames),
             *sems(max(groups, 6)), *sems(CHUNKS + 1), *sems(CHUNKS), *sems(CHUNKS), *sems(PIECES, groups),
             *sems(PIECES), *sems(PIECES, chips), *sems(PIECES, groups),
         ],

time: 47.9 us -> 46 us (0.960)
  local copies, waits for them, and re-layouts: 3.27 us -> 2.01 us
  Pallas kernels: 43.8 us -> 43.2 us
    unnamed x7 -> x3, local copies, waits for them, and re-layouts: 3.27 us -> 2.01 us
    pallas_call x1, Pallas kernels: 43.8 us -> 43.2 us  [body(): pl.pallas_call(functools.partial(kernel, groups, tm), out_shape=(pltpu.VM...]
where the time goes in v4:
time: 46 us; the launch traced here: 45.9 us
  Pallas kernels  43.2 us (94%)
  local copies, waits for them, and re-layouts  2.01 us (4%)
  between operations  0.64 us (1%)
    pallas_call x1, Pallas kernels, body(): pl.pallas_call(functools.partial(kernel, groups, tm), out_shape=(pltpu.VM...  43.2 us
    unnamed x3, local copies, waits for them, and re-layouts  2.01 us

profile of v4, /device:TPU:0, one launch (start us, length us, event | category | flops | bytes accessed | tf_op | source)
XLA Modules:
  0.0 45.9 jit_solution(9720082368930248392)
XLA Ops:
  0.6 43.2 %shard_map.76 = (bf16[128,512]{1,0:T(8,128)(2,1)S(1)}, f32[128,512]{1,0:T(8,128)S(1)}, f32[128,256]{1,0:T(8,128)S(1)}) custom-call(bf16[128,1024]{1,0:T(8,128)(2,1)} %bitcast.7, bf16[1024,512]{1,0:T(8,128)(2,1)} %xw_hbm.1, bf16[1024,256]{1,0:T(8,128)(2,1)} %bw_hbm.1, s32[8,128]{1,0:T(8,128)} %bitcast.9, bf16[128,512]{1,0:T(8,128)(2,1)} %bitcast.8), custom_call_target="tpu_custom_call" | custom-call | tf_op jit(solution)/shard_map/pallas_call | solution.py:344
  43.9 0.7 %copy.11 = bf16[1,128,512]{2,1,0:T(8,128)(2,1)} copy(bf16[1,128,512]{2,1,0:T(8,128)(2,1)S(1)} %bitcast.6) | data formatting | bytes 262144
  44.5 0.7 %copy.13 = f32[128,256]{1,0:T(8,128)} copy(f32[128,256]{1,0:T(8,128)S(1)} %get-tuple-element.11) | data formatting | bytes 262144
  45.2 0.7 %copy.12 = f32[128,512]{1,0:T(8,128)} copy(f32[128,512]{1,0:T(8,128)S(1)} %get-tuple-element.10) | data formatting | bytes 524288

commit v5 on v4

--- a/solution.py
+++ b/solution.py
@@ -89,8 +89,8 @@
         across = lax.rem(d + 2, groups)
         first_a = send_rec(0, d, 0, beside)
         first_b = send_rec(1, d, 1, across)
-        send_rec(2, d, 1, beside)
-        send_rec(3, d, 0, across)
+        second_b = send_rec(2, d, 1, beside, False)
+        second_a = send_rec(3, d, 0, across, False)
         relay_a = send_rec(4, beside, 0, across, False)
         relay_b = send_rec(5, across, 1, beside, False)
     else:
@@ -159,6 +159,9 @@
         passes.append(remote(hop_in.at[at], passed.at[at], p_s.at[c], p_r.at[c], d, partner))
     for copy in exchange:
         copy.start()
+    if square:
+        second_b.start()
+        second_a.start()
 
     def chain(chunks):
         if chunks[0] == 0:

time: 46 us -> 46 us (level)
  no operation moved by 1% of the time
where the time goes in v5:
time: 46 us; the launch traced here: 45.9 us
  Pallas kernels  43.2 us (94%)
  local copies, waits for them, and re-layouts  2.01 us (4%)
  between operations  0.64 us (1%)
    pallas_call x1, Pallas kernels, body(): pl.pallas_call(functools.partial(kernel, groups, tm), out_shape=(pltpu.VM...  43.2 us
    unnamed x3, local copies, waits for them, and re-layouts  2.01 us

profile of v5, /device:TPU:0, one launch (start us, length us, event | category | flops | bytes accessed | tf_op | source)
XLA Modules:
  0.0 45.9 jit_solution(403628015590959169)
XLA Ops:
  0.6 43.2 %shard_map.76 = (bf16[128,512]{1,0:T(8,128)(2,1)S(1)}, f32[128,512]{1,0:T(8,128)S(1)}, f32[128,256]{1,0:T(8,128)S(1)}) custom-call(bf16[128,1024]{1,0:T(8,128)(2,1)} %bitcast.7, bf16[1024,512]{1,0:T(8,128)(2,1)} %xw_hbm.1, bf16[1024,256]{1,0:T(8,128)(2,1)} %bw_hbm.1, s32[8,128]{1,0:T(8,128)} %bitcast.9, bf16[128,512]{1,0:T(8,128)(2,1)} %bitcast.8), custom_call_target="tpu_custom_call" | custom-call | tf_op jit(solution)/shard_map/pallas_call | solution.py:347
  43.9 0.7 %copy.11 = bf16[1,128,512]{2,1,0:T(8,128)(2,1)} copy(bf16[1,128,512]{2,1,0:T(8,128)(2,1)S(1)} %bitcast.6) | data formatting | bytes 262144
  44.5 0.7 %copy.13 = f32[128,256]{1,0:T(8,128)} copy(f32[128,256]{1,0:T(8,128)S(1)} %get-tuple-element.11) | data formatting | bytes 262144
  45.2 0.7 %copy.12 = f32[128,512]{1,0:T(8,128)} copy(f32[128,512]{1,0:T(8,128)S(1)} %get-tuple-element.10) | data formatting | bytes 524288

commit v6 on v5

--- a/solution.py
+++ b/solution.py
@@ -9,7 +9,7 @@
 
 MESH = pl.DeviceIdType.MESH
 CHUNKS = 8
-PIECES = 3
+PIECES = 6
 f32 = jnp.float32
 bf16 = jnp.bfloat16
 
@@ -243,7 +243,8 @@
 
     split = groups * piece
     adjs, carries = [], []
-    for q in range(PIECES - 1):
+    early_pieces = width // split
+    for q in range(early_pieces):
         at = slice(q * split, (q + 1) * split)
         chunks = range(q * split // part, (q + 1) * split // part)
         pl.when(late)(functools.partial(chain, chunks))
@@ -260,7 +261,8 @@
     read_grad = read_local + dot(carry_b, cot_dec, 0, 0)
     gt[width:width + state] = rounded(inj_grad)
     gt[width + state:width + 2 * state] = rounded(read_grad)
-    send_g(PIECES - 1)
+    for q in range(early_pieces, PIECES):
+        send_g(q)
     y_ref[...] = (
         jnp.exp(-unit * run) * dot(readout, carry_b, 1, 1) + ylocal[...]
     ).astype(bf16)

time: 46 us -> 48.6 us (1.057)
  Pallas kernels: 43.2 us -> 45.8 us
    pallas_call x1, Pallas kernels: 43.2 us -> 45.8 us  [body(): pl.pallas_call(functools.partial(kernel, groups, tm), out_shape=(pltpu.VM...]
where the time goes in v6:
time: 48.6 us; the launch traced here: 48.5 us
  Pallas kernels  45.8 us (94%)
  local copies, waits for them, and re-layouts  2.01 us (4%)
  between operations  0.64 us (1%)
    pallas_call x1, Pallas kernels, body(): pl.pallas_call(functools.partial(kernel, groups, tm), out_shape=(pltpu.VM...  45.8 us
    unnamed x3, local copies, waits for them, and re-layouts  2.01 us

profile of v6, /device:TPU:0, one launch (start us, length us, event | category | flops | bytes accessed | tf_op | source)
XLA Modules:
  0.0 48.5 jit_solution(14048322829456235497)
XLA Ops:
  0.6 45.8 %shard_map.76 = (bf16[128,512]{1,0:T(8,128)(2,1)S(1)}, f32[128,512]{1,0:T(8,128)S(1)}, f32[128,256]{1,0:T(8,128)S(1)}) custom-call(bf16[128,1024]{1,0:T(8,128)(2,1)} %bitcast.7, bf16[1024,512]{1,0:T(8,128)(2,1)} %xw_hbm.1, bf16[1024,256]{1,0:T(8,128)(2,1)} %bw_hbm.1, s32[8,128]{1,0:T(8,128)} %bitcast.9, bf16[128,512]{1,0:T(8,128)(2,1)} %bitcast.8), custom_call_target="tpu_custom_call" | custom-call | tf_op jit(solution)/shard_map/pallas_call | solution.py:349
  46.5 0.7 %copy.11 = bf16[1,128,512]{2,1,0:T(8,128)(2,1)} copy(bf16[1,128,512]{2,1,0:T(8,128)(2,1)S(1)} %bitcast.6) | data formatting | bytes 262144
  47.1 0.7 %copy.13 = f32[128,256]{1,0:T(8,128)} copy(f32[128,256]{1,0:T(8,128)S(1)} %get-tuple-element.11) | data formatting | bytes 262144
  47.8 0.7 %copy.12 = f32[128,512]{1,0:T(8,128)} copy(f32[128,512]{1,0:T(8,128)S(1)} %get-tuple-element.10) | data formatting | bytes 524288

commit v7 on v5

--- a/solution.py
+++ b/solution.py
@@ -306,10 +306,10 @@
             o_copies.append(copy)
 
     for step in range(PIECES + 2):
+        if 1 <= step <= PIECES:
+            over_chips(step - 1)
         if step < PIECES:
             product(step)
-        if 1 <= step <= PIECES:
-            over_chips(step - 1)
         if step >= 2:
             over_groups(step - 2)
     for copy in o_copies:

time: 46 us -> 45.2 us (0.983)
  Pallas kernels: 43.2 us -> 42.4 us
    pallas_call x1, Pallas kernels: 43.2 us -> 42.4 us  [body(): pl.pallas_call(functools.partial(kernel, groups, tm), out_shape=(pltpu.VM...]
where the time goes in v7:
time: 45.2 us; the launch traced here: 45 us
  Pallas kernels  42.4 us (94%)
  local copies, waits for them, and re-layouts  2.01 us (4%)
  between operations  0.64 us (1%)
    pallas_call x1, Pallas kernels, body(): pl.pallas_call(functools.partial(kernel, groups, tm), out_shape=(pltpu.VM...  42.4 us
    unnamed x3, local copies, waits for them, and re-layouts  2.01 us

profile of v7, /device:TPU:0, one launch (start us, length us, event | category | flops | bytes accessed | tf_op | source)
XLA Modules:
  0.0 45.0 jit_solution(14062541965693766910)
XLA Ops:
  0.6 42.4 %shard_map.76 = (bf16[128,512]{1,0:T(8,128)(2,1)S(1)}, f32[128,512]{1,0:T(8,128)S(1)}, f32[128,256]{1,0:T(8,128)S(1)}) custom-call(bf16[128,1024]{1,0:T(8,128)(2,1)} %bitcast.7, bf16[1024,512]{1,0:T(8,128)(2,1)} %xw_hbm.1, bf16[1024,256]{1,0:T(8,128)(2,1)} %bw_hbm.1, s32[8,128]{1,0:T(8,128)} %bitcast.9, bf16[128,512]{1,0:T(8,128)(2,1)} %bitcast.8), custom_call_target="tpu_custom_call" | custom-call | tf_op jit(solution)/shard_map/pallas_call | solution.py:347
  43.0 0.7 %copy.11 = bf16[1,128,512]{2,1,0:T(8,128)(2,1)} copy(bf16[1,128,512]{2,1,0:T(8,128)(2,1)S(1)} %bitcast.6) | data formatting | bytes 262144
  43.7 0.7 %copy.13 = f32[128,256]{1,0:T(8,128)} copy(f32[128,256]{1,0:T(8,128)S(1)} %get-tuple-element.11) | data formatting | bytes 262144
  44.3 0.7 %copy.12 = f32[128,512]{1,0:T(8,128)} copy(f32[128,512]{1,0:T(8,128)S(1)} %get-tuple-element.10) | data formatting | bytes 524288
